TPU v7x, 32 devices: a whole 2x2x4 slice. The times are simulated.
32 devices in a mesh: dp: 4 (over y, core), expert: 8 (over z, x).
Axes of the slice: x: 2, y: 2, z: 4, core: 2. Of those that a mesh axis runs over, the one named last changes fastest.
Arguments:
- tokens: bfloat16 [384, 7168], P('expert'), may hold values from -6 to 6
- grad_out: bfloat16 [384, 7168], P('expert'), may hold values from -6 to 6
- routes: int32 [384, 2], P('expert'), may hold values from 0 to 7, all different within a row; in each aligned block of 48 rows (0 to 47, 48 to 95, ...) at most 15 rows name the same one
- gates: bfloat16 [384, 2], P('expert'), may hold values from 0.049804688 to 0.59765625
- w_gate: bfloat16 [8, 7168, 1024], P('expert', None, 'dp'), may hold values from -0.0625 to 0.0625
- w_up: bfloat16 [8, 7168, 1024], P('expert', None, 'dp'), may hold values from -0.0625 to 0.0625
- w_down: bfloat16 [8, 1024, 7168], P('expert', 'dp'), may hold values from -0.1875 to 0.1875
Outputs:
- grad_tokens: bfloat16 [384, 7168], P('expert', 'dp')
- grad_gates: float32 [384, 2], P('expert')
- grad_w_gate: bfloat16 [8, 7168, 1024], P('expert', None, 'dp')
- grad_w_up: bfloat16 [8, 7168, 1024], P('expert', None, 'dp')
- grad_w_down: bfloat16 [8, 1024, 7168], P('expert', 'dp')
Inputs may be any that keep to these rules, and one draw needn't show every extreme that they name: `routes`: within each aligned block of 48 tokens no expert is named by more than 15 pairs, a bound that some block reaches; the 2 experts of one token differ.
All inputs are finite; a program needn't handle non-finite values.
Results may differ from a plain program's by a relative error of at most 0.02.
Values may be sent and summed in bfloat16 or wider, within the bound.
A program may use at most 128 MiB of HBM per device.

v0:
```python
import jax
import jax.numpy as jnp
from jax import lax
from jax.sharding import PartitionSpec as P


def on_device(tokens, grad_out, routes, gates, w_gate, w_up, w_down):
    experts = lax.axis_size("expert")
    groups = lax.axis_size("dp")
    tok_rows = tokens.shape[0]
    width_full = tokens.shape[1]
    top = routes.shape[1]
    cap = tok_rows * top * 5 // (experts * 4)
    slots = experts * cap
    width = width_full // groups
    flat = routes.reshape(-1)
    onehot = (flat[:, None] == jnp.arange(experts, dtype=jnp.int32)[None, :]).astype(jnp.int32)
    earlier = jnp.cumsum(onehot, axis=0) - onehot
    position = jnp.sum(earlier * onehot, axis=1)
    slot_of = (flat * cap + position).reshape(tok_rows, top)
    match = slot_of[None, :, :] == jnp.arange(slots, dtype=jnp.int32)[:, None, None]
    place = jnp.any(match, axis=2).astype(jnp.bfloat16)
    gate_slots = jnp.sum(jnp.where(match, gates.astype(jnp.float32)[None, :, :], 0.0), axis=(1, 2))
    gate_slots = gate_slots.astype(jnp.bfloat16).reshape(experts, cap)

    def fill(source):
        filled = jnp.dot(place, source, preferred_element_type=jnp.float32).astype(jnp.bfloat16)
        return filled.reshape(experts, cap, source.shape[1])

    recv_in, recv_grad, recv_gate = (
        lax.all_to_all(fill(tokens), "expert", split_axis=0, concat_axis=0, tiled=True),
        lax.all_to_all(fill(grad_out), "expert", split_axis=0, concat_axis=0, tiled=True),
        lax.all_to_all(gate_slots, "expert", split_axis=0, concat_axis=0, tiled=True),
    )
    expert_in = recv_in.reshape(slots, width_full)
    expert_grad = recv_grad.reshape(slots, width_full)
    weight_col = recv_gate.reshape(slots).astype(jnp.float32)[:, None]
    gate_mat = w_gate[0]
    up_mat = w_up[0]
    down_mat = w_down[0]
    contract_last = (((1,), (1,)), ((), ()))
    contract_first = (((0,), (0,)), ((), ()))
    pre_gate = jnp.dot(expert_in, gate_mat, preferred_element_type=jnp.float32)
    pre_up = jnp.dot(expert_in, up_mat, preferred_element_type=jnp.float32)
    sigmoid_gate = jax.nn.sigmoid(pre_gate)
    activated = pre_gate * sigmoid_gate
    hidden = activated * pre_up
    stored = hidden.astype(jnp.bfloat16)
    back = lax.dot_general(expert_grad, down_mat, contract_last, preferred_element_type=jnp.float32)
    gate_terms = jnp.sum(stored.astype(jnp.float32) * back, axis=1)
    scaled = (weight_col * hidden).astype(jnp.bfloat16)
    grad_down = lax.dot_general(
        scaled, expert_grad, contract_first, preferred_element_type=jnp.float32
    ).astype(jnp.bfloat16)
    weighted = weight_col * back
    d_up = (weighted * activated).astype(jnp.bfloat16)
    d_gate = (weighted * pre_up * sigmoid_gate * (1.0 + pre_gate * (1.0 - sigmoid_gate))).astype(
        jnp.bfloat16
    )
    grad_gate = lax.dot_general(
        expert_in, d_gate, contract_first, preferred_element_type=jnp.float32
    ).astype(jnp.bfloat16)
    grad_up = lax.dot_general(
        expert_in, d_up, contract_first, preferred_element_type=jnp.float32
    ).astype(jnp.bfloat16)
    gate_total = lax.psum(gate_terms, "dp")
    first = lax.dot_general(gate_mat, d_gate, contract_last, preferred_element_type=jnp.float32)
    summed = lax.psum_scatter(
        (
            first + lax.dot_general(up_mat, d_up, contract_last, preferred_element_type=jnp.float32)
        ).astype(jnp.bfloat16),
        "dp",
        scatter_dimension=0,
        tiled=True,
    ).astype(jnp.float32)
    rows_back, gates_back = (
        lax.all_to_all(
            summed.reshape(width, experts, cap).astype(jnp.bfloat16),
            "expert",
            split_axis=1,
            concat_axis=1,
            tiled=True,
        ).astype(jnp.float32),
        lax.all_to_all(
            gate_total.reshape(1, experts, cap).astype(jnp.bfloat16),
            "expert",
            split_axis=1,
            concat_axis=1,
            tiled=True,
        ).astype(jnp.float32),
    )
    token_grad = lax.dot_general(
        place.astype(jnp.float32),
        rows_back.reshape(width, slots),
        (((0,), (1,)), ((), ())),
        precision=lax.Precision.HIGHEST,
        preferred_element_type=jnp.float32,
    )
    gate_flat = gates_back.reshape(slots)
    grad_gates = jnp.sum(jnp.where(match, gate_flat[:, None, None], 0.0), axis=0)
    return (
        token_grad.astype(jnp.bfloat16),
        grad_gates,
        grad_gate[None],
        grad_up[None],
        grad_down[None],
    )


def solution(mesh):
    placed = (
        P("expert", None),
        P("expert", None),
        P("expert", None),
        P("expert", None),
        P("expert", None, "dp"),
        P("expert", None, "dp"),
        P("expert", "dp", None),
    )
    return jax.shard_map(
        on_device,
        mesh=mesh,
        in_specs=placed,
        out_specs=(
            P("expert", "dp"),
            P("expert", None),
            P("expert", None, "dp"),
            P("expert", None, "dp"),
            P("expert", "dp", None),
        ),
        check_vma=False,
    )
```

profile of v0, /device:TPU:0, one launch (start us, length us, event | category | flops | bytes accessed | tf_op | source)
XLA Modules:
  0.0 203.4 jit_solution(7037050256204612789)
XLA Ops:
  7.2 0.0 copy-start
  7.2 0.8 copy.32
  8.0 0.1 eq.28
  8.1 0.1 fusion.18
  8.2 0.1 reduce_window_sum.11
  8.4 0.2 select_reduce_fusion.2
  8.5 0.1 reduce_sum.39
  8.7 0.1 copy.33
  8.7 0.7 multiply_add_fusion
  9.4 0.1 fusion.17
  9.5 0.7 convolution_convert_fusion.3
  10.2 0.0 copy-start.3
  10.2 1.8 reshape.77
  12.1 7.3 %all-to-all-start.2 = ((bf16[8,15,7168]{2,1,0:T(8,128)(2,1)}), bf16[8,15,7168]{2,1,0:T(8,128)(2,1)}, u32[]{:S(2)}, u32[]{:S(2)}) async-start(bf16[8,15,7168]{2,1,0:T(8,128)(2,1)} %reshape.77), calls=%async_computation.2 | async-start | bytes 3670016 | tf_op jit(solution)/shard_map/all_to_all | solution.py:31
  19.3 0.7 convolution_convert_fusion.4
  20.0 1.8 reshape.75
  21.8 40.2 %all-to-all-done.2 = bf16[8,15,7168]{2,1,0:T(8,128)(2,1)} async-done(((bf16[8,15,7168]{2,1,0:T(8,128)(2,1)}), bf16[8,15,7168]{2,1,0:T(8,128)(2,1)}, u32[]{:S(2)}, u32[]{:S(2)}) %all-to-all-start.2) | async-done | bytes 1720352 | tf_op jit(solution)/shard_map/all_to_all | solution.py:31
  62.0 4.3 %all-to-all-start.1 = ((bf16[8,15,7168]{2,1,0:T(8,128)(2,1)}), bf16[8,15,7168]{2,1,0:T(8,128)(2,1)}, u32[]{:S(2)}, u32[]{:S(2)}) async-start(bf16[8,15,7168]{2,1,0:T(8,128)(2,1)} %reshape.75), calls=%async_computation.1 | async-start | bytes 3670016 | tf_op jit(solution)/shard_map/all_to_all | solution.py:32
  66.3 2.1 %reshape.78 = bf16[120,7168]{1,0:T(8,128)(2,1)S(1)} reshape(bf16[8,15,7168]{2,1,0:T(8,128)(2,1)} %all-to-all-done.2) | data formatting | bytes 3440640 | tf_op jit(solution)/shard_map/reshape | solution.py:35
  68.5 2.8 %fusion.7 = f32[120,256]{1,0:T(8,128)S(1)} fusion(bf16[120,7168]{1,0:T(8,128)(2,1)S(1)} %reshape.78, bf16[1,7168,256]{2,1,0:T(8,128)(2,1)} %param.11), kind=kOutput, calls=%fused_computation.13 | convolution fusion | flops 440401920 | bytes 5513216 | tf_op jit(solution)/shard_map/dot_general | solution.py:43
  71.3 0.3 copy-done.1
  71.6 0.7 fusion.10
  72.4 36.2 %all-to-all-done.1 = bf16[8,15,7168]{2,1,0:T(8,128)(2,1)} async-done(((bf16[8,15,7168]{2,1,0:T(8,128)(2,1)}), bf16[8,15,7168]{2,1,0:T(8,128)(2,1)}, u32[]{:S(2)}, u32[]{:S(2)}) %all-to-all-start.1) | async-done | bytes 1720352 | tf_op jit(solution)/shard_map/all_to_all | solution.py:32
  108.6 3.3 %reshape.76 = bf16[120,7168]{1,0:T(8,128)(2,1)} reshape(bf16[8,15,7168]{2,1,0:T(8,128)(2,1)} %all-to-all-done.1) | data formatting | bytes 3440640 | tf_op jit(solution)/shard_map/reshape | solution.py:36
  111.9 4.0 %multiply_reduce_fusion = (f32[120]{0:T(128)S(1)}, f32[120,256]{1,0:T(8,128)S(1)}) fusion(f32[120,256]{1,0:T(8,128)S(1)} %fusion.10, f32[120,256]{1,0:T(8,128)S(1)} %fusion.7, bf16[120,7168]{1,0:T(8,128)(2,1)} %reshape.76, bf16[1,256,7168]{2,1,0:T(8,128)(2,1)} %param.13), kind=kOutput, calls=%fused_computation.22 | convolution fusion | flops 440678272 | bytes 5759456 | tf_op jit(solution)/shard_map/dot_general | solution.py:49
  115.9 5.7 %psum.7 = bf16[120]{0:T(256)(128)(2,1)S(1)} all-reduce(f32[120]{0:T(128)S(1)} %get-tuple-element.9), channel_id=1, replica_groups=mesh['dp'=4,'expert'=8] {'dp'}, use_global_device_ids=true, to_apply=%region_6.7 | all-reduce | flops 120 | bytes 720 | tf_op jit(solution)/shard_map/psum | solution.py:66
  121.6 0.7 convert_element_type.116
  122.3 4.9 %all-to-all-start.4 = ((bf16[1,8,15]{2,0,1:T(2,128)(2,1)}), bf16[1,8,15]{2,0,1:T(2,128)(2,1)S(1)}, u32[]{:S(2)}, u32[]{:S(2)}) async-start(bf16[1,8,15]{2,0,1:T(2,128)(2,1)} %convert_element_type.116), calls=%async_computation.5 | async-start | bytes 8192 | tf_op jit(solution)/shard_map/all_to_all | solution.py:84
  127.1 0.0 reduce-scatter.2.cloned.1.call-start
  127.2 6.3 %all-to-all-done.4 = bf16[1,8,15]{2,0,1:T(2,128)(2,1)S(1)} async-done(((bf16[1,8,15]{2,0,1:T(2,128)(2,1)}), bf16[1,8,15]{2,0,1:T(2,128)(2,1)S(1)}, u32[]{:S(2)}, u32[]{:S(2)}) %all-to-all-start.4) | async-done | bytes 272 | tf_op jit(solution)/shard_map/all_to_all | solution.py:84
  133.6 0.1 reshape.81
  133.6 0.7 select_reduce_fusion
  134.4 0.1 convert_element_type.115
  134.4 8.8 %all_to_all.26 = bf16[8,1,15]{2,1,0:T(2,128)(2,1)S(1)} all-to-all(bf16[8,1,15]{2,1,0:T(2,128)(2,1)S(1)} %convert_element_type.115), channel_id=1, replica_groups=mesh['dp'=4,'expert'=8] {'expert'}, dimensions={0} | all-to-all | bytes 480 | tf_op jit(solution)/shard_map/all_to_all | solution.py:33
  143.3 0.1 reshape.80
  143.4 0.1 multiply_convert_fusion.1
  143.5 3.4 %fusion.5 = f32[120,7168]{1,0:T(8,128)S(1)} fusion(bf16[120,256]{1,0:T(8,128)(2,1)S(1)} %get-tuple-element.8, bf16[1,7168,256]{2,1,0:T(8,128)(2,1)} %param.11), kind=kOutput, calls=%fused_computation.11 | convolution fusion | flops 440401920 | bytes 7172096 | tf_op jit(solution)/shard_map/dot_general | solution.py:67
  147.0 2.5 %fusion.4 = bf16[7168,120]{0,1:T(8,128)(2,1)} fusion(f32[120,7168]{1,0:T(8,128)S(1)} %fusion.5, bf16[120,256]{1,0:T(8,128)(2,1)S(1)} %get-tuple-element.7, bf16[1,7168,256]{2,1,0:T(8,128)(2,1)S(1)} %copy-done.2), kind=kOutput, calls=%fused_computation.10 | convolution fusion | flops 442122240 | bytes 8892416 | tf_op jit(solution)/shard_map/dot_general | solution.py:70
  149.4 0.0 reduce-scatter.2.cloned.1.call-update
  149.5 25.6 %reduce-scatter.2.cloned.1.call-done = bf16[1792,120]{0,1:T(8,128)(2,1)} async-done(((bf16[7168,120]{0,1:T(8,128)(2,1)}), bf16[1792,120]{0,1:T(8,128)(2,1)}) %reduce-scatter.2.cloned.1.call-update) | async-done | bytes 430096 | tf_op jit(solution)/shard_map/reduce_scatter | solution.py:68
  175.1 1.9 convert_element_type.104
  177.0 5.5 %all-to-all-start.3 = ((bf16[1792,8,15]{0,2,1:T(8,128)(2,1)}), bf16[1792,8,15]{0,2,1:T(8,128)(2,1)S(1)}, u32[]{:S(2)}, u32[]{:S(2)}) async-start(bf16[1792,8,15]{0,2,1:T(8,128)(2,1)} %convert_element_type.104), calls=%async_computation.4 | async-start | bytes 917504 | tf_op jit(solution)/shard_map/all_to_all | solution.py:77
  182.5 4.5 %fusion.2 = bf16[1,256,7168]{2,1,0:T(8,128)(2,1)} fusion(bf16[120,7168]{1,0:T(8,128)(2,1)} %reshape.76, f32[120]{0:T(128)S(1)} %reshape.80, f32[120,256]{1,0:T(8,128)S(1)} %fusion.10, f32[120,256]{1,0:T(8,128)S(1)} %fusion.7), kind=kOutput, calls=%fused_computation.5 | convolution fusion | flops 442451968 | bytes 5636576 | tf_op jit(solution)/shard_map/dot_general | solution.py:52
  187.0 3.0 %fusion.1 = bf16[1,7168,256]{2,1,0:T(8,128)(2,1)} fusion(bf16[120,7168]{1,0:T(8,128)(2,1)S(1)} %reshape.78, bf16[120,256]{1,0:T(8,128)(2,1)S(1)} %get-tuple-element.7), kind=kOutput, calls=%fused_computation.4 | convolution fusion | flops 442236928 | bytes 5451776 | tf_op jit(solution)/shard_map/dot_general | solution.py:63
  190.0 3.0 %fusion = bf16[1,7168,256]{2,1,0:T(8,128)(2,1)} fusion(bf16[120,7168]{1,0:T(8,128)(2,1)S(1)} %reshape.78, bf16[120,256]{1,0:T(8,128)(2,1)S(1)} %get-tuple-element.8), kind=kOutput, calls=%fused_computation.3 | convolution fusion | flops 442236928 | bytes 5451776 | tf_op jit(solution)/shard_map/dot_general | solution.py:60
  193.0 2.6 %all-to-all-done.3 = bf16[1792,8,15]{0,2,1:T(8,128)(2,1)S(1)} async-done(((bf16[1792,8,15]{0,2,1:T(8,128)(2,1)}), bf16[1792,8,15]{0,2,1:T(8,128)(2,1)S(1)}, u32[]{:S(2)}, u32[]{:S(2)}) %all-to-all-start.3) | async-done | bytes 430112 | tf_op jit(solution)/shard_map/all_to_all | solution.py:77
  195.6 0.1 reshape.79
  195.7 0.9 convolution_convert_fusion.5
  (10 shorter events, 0.1 us)
Async XLA Ops:
  7.2 2.4 %copy-start = (bf16[48,7168]{1,0:T(8,128)(2,1)S(1)}, bf16[48,7168]{1,0:T(8,128)(2,1)}, u32[]{:S(2)}) copy-start(bf16[48,7168]{1,0:T(8,128)(2,1)} %param.7) | copy-start | bytes 2064388
  10.2 9.1 %copy-start.3 = (bf16[48,7168]{1,0:T(8,128)(2,1)S(1)}, bf16[48,7168]{1,0:T(8,128)(2,1)}, u32[]{:S(2)}) copy-start(bf16[48,7168]{1,0:T(8,128)(2,1)} %param.8) | copy-start | bytes 2064388
  12.1 50.0 %all-to-all-start.2 = ((bf16[8,15,7168]{2,1,0:T(8,128)(2,1)}), bf16[8,15,7168]{2,1,0:T(8,128)(2,1)}, u32[]{:S(2)}, u32[]{:S(2)}) async-start(bf16[8,15,7168]{2,1,0:T(8,128)(2,1)} %reshape.77), calls=%async_computation.2 | async-start | bytes 3670016 | tf_op jit(solution)/shard_map/all_to_all | solution.py:31
  62.0 46.6 %all-to-all-start.1 = ((bf16[8,15,7168]{2,1,0:T(8,128)(2,1)}), bf16[8,15,7168]{2,1,0:T(8,128)(2,1)}, u32[]{:S(2)}, u32[]{:S(2)}) async-start(bf16[8,15,7168]{2,1,0:T(8,128)(2,1)} %reshape.75), calls=%async_computation.1 | async-start | bytes 3670016 | tf_op jit(solution)/shard_map/all_to_all | solution.py:32
  68.5 3.1 %copy-start.1 = (bf16[1,7168,256]{2,1,0:T(8,128)(2,1)S(1)}, bf16[1,7168,256]{2,1,0:T(8,128)(2,1)}, u32[]{:S(2)}) copy-start(bf16[1,7168,256]{2,1,0:T(8,128)(2,1)} %param.12) | copy-start | bytes 11010052
  111.9 15.3 %copy-start.4 = (bf16[48,2]{0,1:T(2,128)(2,1)S(1)}, bf16[48,2]{0,1:T(2,128)(2,1)}, u32[]{:S(2)}) copy-start(bf16[48,2]{0,1:T(2,128)(2,1)} %param.10) | copy-start | bytes 580
  122.3 11.2 %all-to-all-start.4 = ((bf16[1,8,15]{2,0,1:T(2,128)(2,1)}), bf16[1,8,15]{2,0,1:T(2,128)(2,1)S(1)}, u32[]{:S(2)}, u32[]{:S(2)}) async-start(bf16[1,8,15]{2,0,1:T(2,128)(2,1)} %convert_element_type.116), calls=%async_computation.5 | async-start | bytes 8192 | tf_op jit(solution)/shard_map/all_to_all | solution.py:84
  127.1 47.9 %reduce-scatter.2.cloned.1.call-start = ((), (), s32[]{:S(2)}) async-start(), calls=%async_computation.6 | async-start | bytes 2150400 | tf_op jit(solution)/shard_map/reduce_scatter | solution.py:68
  143.5 3.5 %copy-start.2 = (bf16[1,7168,256]{2,1,0:T(8,128)(2,1)S(1)}, bf16[1,7168,256]{2,1,0:T(8,128)(2,1)}, u32[]{:S(2)}) copy-start(bf16[1,7168,256]{2,1,0:T(8,128)(2,1)} %param.12) | copy-start | bytes 11010052
  177.0 18.6 %all-to-all-start.3 = ((bf16[1792,8,15]{0,2,1:T(8,128)(2,1)}), bf16[1792,8,15]{0,2,1:T(8,128)(2,1)S(1)}, u32[]{:S(2)}, u32[]{:S(2)}) async-start(bf16[1792,8,15]{0,2,1:T(8,128)(2,1)} %convert_element_type.104), calls=%async_computation.4 | async-start | bytes 917504 | tf_op jit(solution)/shard_map/all_to_all | solution.py:77
Sparse Core Ops, SparseCore 0:
  149.6 25.4 reduce-scatter.1
where the time goes:
time: 204 us; the launch traced here: 203 us
  waiting for transfers between devices  111 us (54%)
  matrix products  26.2 us (13%)
  starting transfers between devices  22 us (11%)
  blocking collectives  14.5 us (7%)
  between operations  14.2 us (7%)
  local copies, waits for them, and re-layouts  13.6 us (7%)
  other arithmetic  2.05 us (1%)
    all_to_all x1, waiting for transfers between devices, on_device(): lax.all_to_all(fill(tokens), 'expert', split_axis=0, concat_axis=0, tiled...  40.2 us
    all_to_all x1, waiting for transfers between devices, on_device(): lax.all_to_all(fill(grad_out), 'expert', split_axis=0, concat_axis=0, til...  36.2 us
    reduce_scatter x1, waiting for transfers between devices, on_device(): lax.psum_scatter((first + lax.dot_general(up_mat, d_up, contract_last, pr...  25.6 us
    all_to_all x1, blocking collectives, on_device(): lax.all_to_all(gate_slots, 'expert', split_axis=0, concat_axis=0, tiled=T...  8.82 us
    all_to_all x1, starting transfers between devices, on_device(): lax.all_to_all(fill(tokens), 'expert', split_axis=0, concat_axis=0, tiled...  7.25 us
    all_to_all x1, waiting for transfers between devices, on_device(): lax.all_to_all(gate_total.reshape(1, experts, cap).astype(jnp.bfloat16),...  6.32 us
    psum x1, blocking collectives, on_device(): gate_total = lax.psum(gate_terms, 'dp')  5.68 us
    all_to_all x1, starting transfers between devices, on_device(): lax.all_to_all(summed.reshape(width, experts, cap).astype(jnp.bfloat16),...  5.51 us
  transfers between devices with their start and end apart: 5, of which 5 were waited for; matrix products, arithmetic and copies ran while one was open for 9% of the time, Pallas kernels for 0%

commit v1 on v0

--- a/solution.py
+++ b/solution.py
@@ -2,6 +2,22 @@
 import jax.numpy as jnp
 from jax import lax
 from jax.sharding import PartitionSpec as P
+
+
+def swapped_with_each(x, axis, split, join):
+    ways, here = (lax.axis_size(axis), lax.axis_index(axis))
+    width = x.shape[split] // ways
+    dims = list(x.shape)
+    dims[split] = width
+    height = dims[join]
+    dims[join] = height * ways
+    full = jnp.zeros(dims, x.dtype)
+    for mask in range(ways):
+        part = lax.dynamic_slice_in_dim(x, (here ^ mask) * width, width, axis=split)
+        if mask:
+            part = lax.ppermute(part, axis, [(d, d ^ mask) for d in range(ways)])
+        full = lax.dynamic_update_slice_in_dim(full, part, (here ^ mask) * height, axis=join)
+    return full
 
 
 def on_device(tokens, grad_out, routes, gates, w_gate, w_up, w_down):
@@ -30,7 +46,7 @@
     recv_in, recv_grad, recv_gate = (
         lax.all_to_all(fill(tokens), "expert", split_axis=0, concat_axis=0, tiled=True),
         lax.all_to_all(fill(grad_out), "expert", split_axis=0, concat_axis=0, tiled=True),
-        lax.all_to_all(gate_slots, "expert", split_axis=0, concat_axis=0, tiled=True),
+        swapped_with_each(gate_slots, "expert", 0, 0),
     )
     expert_in = recv_in.reshape(slots, width_full)
     expert_grad = recv_grad.reshape(slots, width_full)

time: 204 us -> 215 us (1.054)
  waiting for transfers between devices: 111 us -> 122 us
  blocking collectives: 14.5 us -> 5.68 us
  starting transfers between devices: 22 us -> 30.2 us
    ppermute x0 -> x7, waiting for transfers between devices: none -> 10.9 us  [swapped_with_each(): part = lax.ppermute(part, axis, [(d, d ^ mask) for d in range(ways)])]
    all_to_all x1 -> x0, blocking collectives: 8.82 us -> none  [on_device(): lax.all_to_all(gate_slots, 'expert', split_axis=0, concat_axis=0, tiled=T...]
    ppermute x0 -> x7, starting transfers between devices: none -> 8.27 us  [swapped_with_each(): part = lax.ppermute(part, axis, [(d, d ^ mask) for d in range(ways)])]
  transfers between devices with their start and end apart: 5 -> 12, of which waited for: 5 -> 8; matrix products, arithmetic and copies ran while one was open for 9% -> 9% of each run, Pallas kernels for 0% -> 0%
where the time goes in v1:
time: 215 us; the launch traced here: 214 us
  waiting for transfers between devices  122 us (57%)
  starting transfers between devices  30.2 us (14%)
  matrix products  26.2 us (12%)
  between operations  14.3 us (7%)
  local copies, waits for them, and re-layouts  13.9 us (6%)
  blocking collectives  5.68 us (3%)
    all_to_all x1, waiting for transfers between devices, on_device(): lax.all_to_all(fill(tokens), 'expert', split_axis=0, concat_axis=0, tiled...  40.2 us
    all_to_all x1, waiting for transfers between devices, on_device(): lax.all_to_all(fill(grad_out), 'expert', split_axis=0, concat_axis=0, til...  36.2 us
    reduce_scatter x1, waiting for transfers between devices, on_device(): lax.psum_scatter((first + lax.dot_general(up_mat, d_up, contract_last, pr...  25.6 us
    ppermute x7, waiting for transfers between devices, swapped_with_each(): part = lax.ppermute(part, axis, [(d, d ^ mask) for d in range(ways)])  10.9 us
    ppermute x7, starting transfers between devices, swapped_with_each(): part = lax.ppermute(part, axis, [(d, d ^ mask) for d in range(ways)])  8.27 us
    all_to_all x1, starting transfers between devices, on_device(): lax.all_to_all(fill(tokens), 'expert', split_axis=0, concat_axis=0, tiled...  7.25 us
    all_to_all x1, waiting for transfers between devices, on_device(): lax.all_to_all(gate_total.reshape(1, experts, cap).astype(jnp.bfloat16),...  6.3 us
    psum x1, blocking collectives, on_device(): gate_total = lax.psum(gate_terms, 'dp')  5.68 us
  transfers between devices with their start and end apart: 12, of which 8 were waited for; matrix products, arithmetic and copies ran while one was open for 9% of the time, Pallas kernels for 0%

profile of v1, /device:TPU:0, one launch (start us, length us, event | category | flops | bytes accessed | tf_op | source)
XLA Modules:
  0.0 214.1 jit_solution(8568150451479390204)
XLA Ops:
  7.2 0.8 copy.30
  8.0 0.1 eq.28
  8.1 0.1 fusion.18
  8.2 0.1 reduce_window_sum.11
  8.4 0.2 select_reduce_fusion.2
  8.5 0.1 reduce_sum.39
  8.7 0.7 multiply_add_fusion
  9.4 0.1 fusion.17
  9.5 0.7 convolution_convert_fusion.3
  10.2 1.8 reshape.64
  12.1 7.3 %all-to-all-start.1 = ((bf16[8,15,7168]{2,1,0:T(8,128)(2,1)}), bf16[8,15,7168]{2,1,0:T(8,128)(2,1)}, u32[]{:S(2)}, u32[]{:S(2)}) async-start(bf16[8,15,7168]{2,1,0:T(8,128)(2,1)} %reshape.64), calls=%async_computation.1 | async-start | bytes 3670016 | tf_op jit(solution)/shard_map/all_to_all | solution.py:47
  19.3 0.7 convolution_convert_fusion.4
  20.0 1.8 reshape.62
  21.8 40.2 %all-to-all-done.1 = bf16[8,15,7168]{2,1,0:T(8,128)(2,1)} async-done(((bf16[8,15,7168]{2,1,0:T(8,128)(2,1)}), bf16[8,15,7168]{2,1,0:T(8,128)(2,1)}, u32[]{:S(2)}, u32[]{:S(2)}) %all-to-all-start.1) | async-done | bytes 1720352 | tf_op jit(solution)/shard_map/all_to_all | solution.py:47
  62.0 4.3 %all-to-all-start = ((bf16[8,15,7168]{2,1,0:T(8,128)(2,1)}), bf16[8,15,7168]{2,1,0:T(8,128)(2,1)}, u32[]{:S(2)}, u32[]{:S(2)}) async-start(bf16[8,15,7168]{2,1,0:T(8,128)(2,1)} %reshape.62), calls=%async_computation | async-start | bytes 3670016 | tf_op jit(solution)/shard_map/all_to_all | solution.py:48
  66.4 2.1 reshape.65
  68.5 2.9 %fusion.7 = f32[120,256]{1,0:T(8,128)S(1)} fusion(bf16[120,7168]{1,0:T(8,128)(2,1)S(1)} %reshape.65, bf16[1,7168,256]{2,1,0:T(8,128)(2,1)} %param.11), kind=kOutput, calls=%fused_computation.13 | convolution fusion | flops 440401920 | bytes 5513216 | tf_op jit(solution)/shard_map/dot_general | solution.py:59
  71.4 0.3 copy-done.1
  71.7 0.7 fusion.10
  72.4 36.2 %all-to-all-done = bf16[8,15,7168]{2,1,0:T(8,128)(2,1)} async-done(((bf16[8,15,7168]{2,1,0:T(8,128)(2,1)}), bf16[8,15,7168]{2,1,0:T(8,128)(2,1)}, u32[]{:S(2)}, u32[]{:S(2)}) %all-to-all-start) | async-done | bytes 1720352 | tf_op jit(solution)/shard_map/all_to_all | solution.py:48
  108.6 3.3 %reshape.63 = bf16[120,7168]{1,0:T(8,128)(2,1)} reshape(bf16[8,15,7168]{2,1,0:T(8,128)(2,1)} %all-to-all-done) | data formatting | bytes 3440640 | tf_op jit(solution)/shard_map/reshape | solution.py:52
  111.9 4.0 %multiply_reduce_fusion = (f32[120]{0:T(128)S(1)}, f32[120,256]{1,0:T(8,128)S(1)}) fusion(f32[120,256]{1,0:T(8,128)S(1)} %fusion.10, f32[120,256]{1,0:T(8,128)S(1)} %fusion.7, bf16[120,7168]{1,0:T(8,128)(2,1)} %reshape.63, bf16[1,256,7168]{2,1,0:T(8,128)(2,1)} %param.13), kind=kOutput, calls=%fused_computation.22 | convolution fusion | flops 440678272 | bytes 5759456 | tf_op jit(solution)/shard_map/dot_general | solution.py:65
  115.9 5.7 %psum.7 = bf16[120]{0:T(256)(128)(2,1)S(1)} all-reduce(f32[120]{0:T(128)S(1)} %get-tuple-element.17), channel_id=1, replica_groups=mesh['dp'=4,'expert'=8] {'dp'}, use_global_device_ids=true, to_apply=%region_6.7 | all-reduce | flops 120 | bytes 720 | tf_op jit(solution)/shard_map/psum | solution.py:82
  121.6 0.7 convert_element_type.108
  122.3 4.9 %all-to-all-start.3 = ((bf16[1,8,15]{2,0,1:T(2,128)(2,1)}), bf16[1,8,15]{2,0,1:T(2,128)(2,1)S(1)}, u32[]{:S(2)}, u32[]{:S(2)}) async-start(bf16[1,8,15]{2,0,1:T(2,128)(2,1)} %convert_element_type.108), calls=%async_computation.4 | async-start | bytes 8192 | tf_op jit(solution)/shard_map/all_to_all | solution.py:100
  127.2 6.3 %all-to-all-done.3 = bf16[1,8,15]{2,0,1:T(2,128)(2,1)S(1)} async-done(((bf16[1,8,15]{2,0,1:T(2,128)(2,1)}), bf16[1,8,15]{2,0,1:T(2,128)(2,1)S(1)}, u32[]{:S(2)}, u32[]{:S(2)}) %all-to-all-start.3) | async-done | bytes 272 | tf_op jit(solution)/shard_map/all_to_all | solution.py:100
  133.6 0.7 select_reduce_fusion
  134.4 0.1 convert_element_type.88
  134.5 0.6 collective-permute-start.6
  135.1 3.2 %collective-permute-start.5 = (bf16[1,15]{1,0:T(2,128)(2,1)S(1)}, bf16[1,15]{1,0:T(2,128)(2,1)S(1)}, u32[]{:S(2)}, u32[]{:S(2)}) collective-permute-start(bf16[1,15]{1,0:T(2,128)(2,1)S(1)} %get-tuple-element.10), channel_id=1, source_target_pairs={{0,6},{1,7},{2,4},{3,5},{4,2},{5,3},{6,0},{7,1},{8,14},{9,15},{10,... | collective-permute-start | bytes 98 | tf_op jit(solution)/shard_map/ppermute | solution.py:18
  138.3 3.8 %collective-permute-start.3 = (bf16[1,15]{1,0:T(2,128)(2,1)S(1)}, bf16[1,15]{1,0:T(2,128)(2,1)S(1)}, u32[]{:S(2)}, u32[]{:S(2)}) collective-permute-start(bf16[1,15]{1,0:T(2,128)(2,1)S(1)} %get-tuple-element.12), channel_id=1, source_target_pairs={{0,4},{1,5},{2,6},{3,7},{4,0},{5,1},{6,2},{7,3},{8,12},{9,13},{10,... | collective-permute-start | bytes 98 | tf_op jit(solution)/shard_map/ppermute | solution.py:18
  142.2 0.6 collective-permute-start
  142.8 3.0 %collective-permute-done = bf16[1,15]{1,0:T(2,128)(2,1)S(1)} collective-permute-done((bf16[1,15]{1,0:T(2,128)(2,1)S(1)}, bf16[1,15]{1,0:T(2,128)(2,1)S(1)}, u32[]{:S(2)}, u32[]{:S(2)}) %collective-permute-start) | collective-permute-done | bytes 62 | tf_op jit(solution)/shard_map/ppermute | solution.py:18
  145.8 3.5 %collective-permute-done.1 = bf16[1,15]{1,0:T(2,128)(2,1)S(1)} collective-permute-done((bf16[1,15]{1,0:T(2,128)(2,1)S(1)}, bf16[1,15]{1,0:T(2,128)(2,1)S(1)}, u32[]{:S(2)}, u32[]{:S(2)}) %collective-permute-start.1) | collective-permute-done | bytes 62 | tf_op jit(solution)/shard_map/ppermute | solution.py:18
  149.3 4.4 %collective-permute-done.2 = bf16[1,15]{1,0:T(2,128)(2,1)S(1)} collective-permute-done((bf16[1,15]{1,0:T(2,128)(2,1)S(1)}, bf16[1,15]{1,0:T(2,128)(2,1)S(1)}, u32[]{:S(2)}, u32[]{:S(2)}) %collective-permute-start.2) | collective-permute-done | bytes 62 | tf_op jit(solution)/shard_map/ppermute | solution.py:18
  153.9 0.1 reshape.67
  154.0 0.1 multiply_convert_fusion.1
  154.1 3.4 %fusion.5 = f32[120,7168]{1,0:T(8,128)S(1)} fusion(bf16[120,256]{1,0:T(8,128)(2,1)S(1)} %get-tuple-element.8, bf16[1,7168,256]{2,1,0:T(8,128)(2,1)} %param.11), kind=kOutput, calls=%fused_computation.11 | convolution fusion | flops 440401920 | bytes 7172096 | tf_op jit(solution)/shard_map/dot_general | solution.py:83
  157.6 2.5 %fusion.4 = bf16[7168,120]{0,1:T(8,128)(2,1)} fusion(f32[120,7168]{1,0:T(8,128)S(1)} %fusion.5, bf16[120,256]{1,0:T(8,128)(2,1)S(1)} %get-tuple-element.7, bf16[1,7168,256]{2,1,0:T(8,128)(2,1)S(1)} %copy-done.2), kind=kOutput, calls=%fused_computation.10 | convolution fusion | flops 442122240 | bytes 8892416 | tf_op jit(solution)/shard_map/dot_general | solution.py:86
  160.1 25.6 %reduce-scatter.2.cloned.1.call-done = bf16[1792,120]{0,1:T(8,128)(2,1)} async-done(((bf16[7168,120]{0,1:T(8,128)(2,1)}), bf16[1792,120]{0,1:T(8,128)(2,1)}) %reduce-scatter.2.cloned.1.call-update) | async-done | bytes 430096 | tf_op jit(solution)/shard_map/reduce_scatter | solution.py:84
  185.7 1.9 convert_element_type.97
  187.6 5.5 %all-to-all-start.2 = ((bf16[1792,8,15]{0,2,1:T(8,128)(2,1)}), bf16[1792,8,15]{0,2,1:T(8,128)(2,1)S(1)}, u32[]{:S(2)}, u32[]{:S(2)}) async-start(bf16[1792,8,15]{0,2,1:T(8,128)(2,1)} %convert_element_type.97), calls=%async_computation.3 | async-start | bytes 917504 | tf_op jit(solution)/shard_map/all_to_all | solution.py:93
  193.1 4.5 %fusion.2 = bf16[1,256,7168]{2,1,0:T(8,128)(2,1)} fusion(bf16[120,7168]{1,0:T(8,128)(2,1)} %reshape.63, f32[120]{0:T(128)S(1)} %reshape.67, f32[120,256]{1,0:T(8,128)S(1)} %fusion.10, f32[120,256]{1,0:T(8,128)S(1)} %fusion.7), kind=kOutput, calls=%fused_computation.5 | convolution fusion | flops 442451968 | bytes 5636576 | tf_op jit(solution)/shard_map/dot_general | solution.py:68
  197.6 3.0 %fusion.1 = bf16[1,7168,256]{2,1,0:T(8,128)(2,1)} fusion(bf16[120,7168]{1,0:T(8,128)(2,1)S(1)} %reshape.65, bf16[120,256]{1,0:T(8,128)(2,1)S(1)} %get-tuple-element.7), kind=kOutput, calls=%fused_computation.4 | convolution fusion | flops 442236928 | bytes 5451776 | tf_op jit(solution)/shard_map/dot_general | solution.py:79
  200.6 3.0 %fusion = bf16[1,7168,256]{2,1,0:T(8,128)(2,1)} fusion(bf16[120,7168]{1,0:T(8,128)(2,1)S(1)} %reshape.65, bf16[120,256]{1,0:T(8,128)(2,1)S(1)} %get-tuple-element.8), kind=kOutput, calls=%fused_computation.3 | convolution fusion | flops 442236928 | bytes 5451776 | tf_op jit(solution)/shard_map/dot_general | solution.py:76
  203.6 2.6 %all-to-all-done.2 = bf16[1792,8,15]{0,2,1:T(8,128)(2,1)S(1)} async-done(((bf16[1792,8,15]{0,2,1:T(8,128)(2,1)}), bf16[1792,8,15]{0,2,1:T(8,128)(2,1)S(1)}, u32[]{:S(2)}, u32[]{:S(2)}) %all-to-all-start.2) | async-done | bytes 430112 | tf_op jit(solution)/shard_map/all_to_all | solution.py:93
  206.2 0.1 reshape.66
  206.3 0.9 convolution_convert_fusion.5
  (32 shorter events, 0.5 us)
Async XLA Ops:
  7.2 2.4 %copy-start = (bf16[48,7168]{1,0:T(8,128)(2,1)S(1)}, bf16[48,7168]{1,0:T(8,128)(2,1)}, u32[]{:S(2)}) copy-start(bf16[48,7168]{1,0:T(8,128)(2,1)} %param.7) | copy-start | bytes 2064388
  10.2 9.1 %copy-start.3 = (bf16[48,7168]{1,0:T(8,128)(2,1)S(1)}, bf16[48,7168]{1,0:T(8,128)(2,1)}, u32[]{:S(2)}) copy-start(bf16[48,7168]{1,0:T(8,128)(2,1)} %param.8) | copy-start | bytes 2064388
  12.1 50.0 %all-to-all-start.1 = ((bf16[8,15,7168]{2,1,0:T(8,128)(2,1)}), bf16[8,15,7168]{2,1,0:T(8,128)(2,1)}, u32[]{:S(2)}, u32[]{:S(2)}) async-start(bf16[8,15,7168]{2,1,0:T(8,128)(2,1)} %reshape.64), calls=%async_computation.1 | async-start | bytes 3670016 | tf_op jit(solution)/shard_map/all_to_all | solution.py:47
  20.0 46.4 %copy-start.4 = (bf16[48,2]{0,1:T(2,128)(2,1)S(1)}, bf16[48,2]{0,1:T(2,128)(2,1)}, u32[]{:S(2)}) copy-start(bf16[48,2]{0,1:T(2,128)(2,1)} %param.10) | copy-start | bytes 580
  62.0 46.6 %all-to-all-start = ((bf16[8,15,7168]{2,1,0:T(8,128)(2,1)}), bf16[8,15,7168]{2,1,0:T(8,128)(2,1)}, u32[]{:S(2)}, u32[]{:S(2)}) async-start(bf16[8,15,7168]{2,1,0:T(8,128)(2,1)} %reshape.62), calls=%async_computation | async-start | bytes 3670016 | tf_op jit(solution)/shard_map/all_to_all | solution.py:48
  68.5 3.1 %copy-start.1 = (bf16[1,7168,256]{2,1,0:T(8,128)(2,1)S(1)}, bf16[1,7168,256]{2,1,0:T(8,128)(2,1)}, u32[]{:S(2)}) copy-start(bf16[1,7168,256]{2,1,0:T(8,128)(2,1)} %param.12) | copy-start | bytes 11010052
  122.3 11.2 %all-to-all-start.3 = ((bf16[1,8,15]{2,0,1:T(2,128)(2,1)}), bf16[1,8,15]{2,0,1:T(2,128)(2,1)S(1)}, u32[]{:S(2)}, u32[]{:S(2)}) async-start(bf16[1,8,15]{2,0,1:T(2,128)(2,1)} %convert_element_type.108), calls=%async_computation.4 | async-start | bytes 8192 | tf_op jit(solution)/shard_map/all_to_all | solution.py:100
  127.1 58.5 %reduce-scatter.2.cloned.1.call-start = ((), (), s32[]{:S(2)}) async-start(), calls=%async_computation.5 | async-start | bytes 2150400 | tf_op jit(solution)/shard_map/reduce_scatter | solution.py:84
  134.5 19.4 %collective-permute-start.6 = (bf16[1,15]{1,0:T(2,128)(2,1)S(1)}, bf16[1,15]{1,0:T(2,128)(2,1)S(1)}, u32[]{:S(2)}, u32[]{:S(2)}) collective-permute-start(bf16[1,15]{1,0:T(2,128)(2,1)S(1)} %get-tuple-element.9), channel_id=1, source_target_pairs={{0,7},{1,6},{2,5},{3,4},{4,3},{5,2},{6,1},{7,0},{8,15},{9,14},{10,... | collective-permute-start | bytes 98 | tf_op jit(solution)/shard_map/ppermute | solution.py:18
  135.1 18.7 %collective-permute-start.5 = (bf16[1,15]{1,0:T(2,128)(2,1)S(1)}, bf16[1,15]{1,0:T(2,128)(2,1)S(1)}, u32[]{:S(2)}, u32[]{:S(2)}) collective-permute-start(bf16[1,15]{1,0:T(2,128)(2,1)S(1)} %get-tuple-element.10), channel_id=1, source_target_pairs={{0,6},{1,7},{2,4},{3,5},{4,2},{5,3},{6,0},{7,1},{8,14},{9,15},{10,... | collective-permute-start | bytes 98 | tf_op jit(solution)/shard_map/ppermute | solution.py:18
  138.3 15.4 %collective-permute-start.4 = (bf16[1,15]{1,0:T(2,128)(2,1)S(1)}, bf16[1,15]{1,0:T(2,128)(2,1)S(1)}, u32[]{:S(2)}, u32[]{:S(2)}) collective-permute-start(bf16[1,15]{1,0:T(2,128)(2,1)S(1)} %get-tuple-element.11), channel_id=1, source_target_pairs={{0,5},{1,4},{2,7},{3,6},{4,1},{5,0},{6,3},{7,2},{8,13},{9,12},{10,... | collective-permute-start | bytes 98 | tf_op jit(solution)/shard_map/ppermute | solution.py:18
  138.3 15.4 %collective-permute-start.3 = (bf16[1,15]{1,0:T(2,128)(2,1)S(1)}, bf16[1,15]{1,0:T(2,128)(2,1)S(1)}, u32[]{:S(2)}, u32[]{:S(2)}) collective-permute-start(bf16[1,15]{1,0:T(2,128)(2,1)S(1)} %get-tuple-element.12), channel_id=1, source_target_pairs={{0,4},{1,5},{2,6},{3,7},{4,0},{5,1},{6,2},{7,3},{8,12},{9,13},{10,... | collective-permute-start | bytes 98 | tf_op jit(solution)/shard_map/ppermute | solution.py:18
  142.2 3.5 %collective-permute-start = (bf16[1,15]{1,0:T(2,128)(2,1)S(1)}, bf16[1,15]{1,0:T(2,128)(2,1)S(1)}, u32[]{:S(2)}, u32[]{:S(2)}) collective-permute-start(bf16[1,15]{1,0:T(2,128)(2,1)S(1)} %get-tuple-element.15), channel_id=1, source_target_pairs={{0,1},{1,0},{2,3},{3,2},{4,5},{5,4},{6,7},{7,6},{8,9},{9,8},{10,11... | collective-permute-start | bytes 98 | tf_op jit(solution)/shard_map/ppermute | solution.py:18
  145.7 3.5 %collective-permute-start.1 = (bf16[1,15]{1,0:T(2,128)(2,1)S(1)}, bf16[1,15]{1,0:T(2,128)(2,1)S(1)}, u32[]{:S(2)}, u32[]{:S(2)}) collective-permute-start(bf16[1,15]{1,0:T(2,128)(2,1)S(1)} %get-tuple-element.14), channel_id=1, source_target_pairs={{0,2},{1,3},{2,0},{3,1},{4,6},{5,7},{6,4},{7,5},{8,10},{9,11},{10,... | collective-permute-start | bytes 98 | tf_op jit(solution)/shard_map/ppermute | solution.py:18
  149.3 4.4 %collective-permute-start.2 = (bf16[1,15]{1,0:T(2,128)(2,1)S(1)}, bf16[1,15]{1,0:T(2,128)(2,1)S(1)}, u32[]{:S(2)}, u32[]{:S(2)}) collective-permute-start(bf16[1,15]{1,0:T(2,128)(2,1)S(1)} %get-tuple-element.13), channel_id=1, source_target_pairs={{0,3},{1,2},{2,1},{3,0},{4,7},{5,6},{6,5},{7,4},{8,11},{9,10},{10,... | collective-permute-start | bytes 98 | tf_op jit(solution)/shard_map/ppermute | solution.py:18
  154.1 3.5 %copy-start.2 = (bf16[1,7168,256]{2,1,0:T(8,128)(2,1)S(1)}, bf16[1,7168,256]{2,1,0:T(8,128)(2,1)}, u32[]{:S(2)}) copy-start(bf16[1,7168,256]{2,1,0:T(8,128)(2,1)} %param.12) | copy-start | bytes 11010052
  187.6 18.6 %all-to-all-start.2 = ((bf16[1792,8,15]{0,2,1:T(8,128)(2,1)}), bf16[1792,8,15]{0,2,1:T(8,128)(2,1)S(1)}, u32[]{:S(2)}, u32[]{:S(2)}) async-start(bf16[1792,8,15]{0,2,1:T(8,128)(2,1)} %convert_element_type.97), calls=%async_computation.3 | async-start | bytes 917504 | tf_op jit(solution)/shard_map/all_to_all | solution.py:93
Sparse Core Ops, SparseCore 0:
  160.2 25.4 reduce-scatter.1
